TPU v7x, 256 devices: a whole 4x4x8 slice. The times are simulated.
256 devices in a mesh: win: 4 (over y_lo, core), tile: 64 (over x, y_hi, z).
Axes of the slice: x: 4, y: 4 (y_hi: 2, y_lo: 2; y = y_hi * 2 + y_lo), z: 8, core: 2. Of those that a mesh axis runs over, the one named last changes fastest.
Arguments:
- state: float32 [4, 64, 5, 32, 8, 128], P('win', 'tile'), may hold values from -6 to 6
- obs_weight: float32 [4, 64, 5, 32, 8, 128], P('win', 'tile'), may hold values from 0 to 1
- trajectory: bfloat16 [4, 64, 3, 2, 32, 8, 128], P('win', 'tile'), may hold values from -0.8984375 to 0.8984375
- coupling: float32 [5, 5], replicated, may hold values from -0.9 to 0.9
- prec_scale: float32 [5, 32], replicated, may hold values from 0.5 to 2
Outputs:
- hess_vec: float32 [4, 64, 5, 32, 8, 128], P('win', 'tile')
All inputs are finite; a program needn't handle non-finite values.
Results may differ from a plain program's by a relative error of at most 0.0003.
Values sent between devices are 32-bit elements; how exact they have to be, the bound alone decides.
No kernel may reach another device: no remote copies, remote signals or barrier semaphores. Data moves between devices by JAX's collectives and lax.ppermute only.
A program may use at most 64 MiB of HBM per device.

v0:
```python
import functools

import jax
import jax.numpy as jnp
from jax import lax
from jax.experimental import pallas as pl
from jax.experimental.pallas import tpu as pltpu
from jax.sharding import PartitionSpec as P

VARS = 5
STEPS = 3
GROUP = 16
HALO = 5
TY = 4
smooth_weight = 0.2


def passed_along(x, axis, by):
    devices = lax.axis_size(axis)
    pairs = [(i, i + by) for i in range(devices) if 0 <= i + by < devices]
    return lax.ppermute(x, axis, pairs)


def shifted(x, axis, by):
    devices = lax.axis_size(axis)
    return lax.ppermute(x, axis, [(i, (i + by) % devices) for i in range(devices)])


def exchange(x):
    groups = [[first + i for i in range(GROUP)] for first in range(0, lax.axis_size("tile"), GROUP)]
    return lax.all_to_all(x, "tile", 0, 0, axis_index_groups=groups, tiled=True)


def masks():
    row = lax.broadcasted_iota(jnp.int32, (8, 128), 0)
    lane = lax.broadcasted_iota(jnp.int32, (8, 128), 1)
    return row == 0, row == 7, lane == 0, lane == 127


def east(sel, here, there):
    return pltpu.roll(jnp.where(sel[0], there, here), 7, 0)


def west(sel, here, there):
    return pltpu.roll(jnp.where(sel[1], there, here), 1, 0)


def north(sel, here, there):
    return pltpu.roll(jnp.where(sel[2], there, here), 127, 1)


def south(sel, here, there):
    return pltpu.roll(jnp.where(sel[3], there, here), 1, 1)


def mixed(coupling, values, a, transposed):
    terms = [(coupling[b, a] if transposed else coupling[a, b]) * values[b] for b in range(VARS)]
    return ((terms[0] + terms[1]) + (terms[2] + terms[3])) + terms[4]


class Slab:
    def __init__(self, parts, first=0):
        self.parts, self.first = parts, first

    def __getitem__(self, at):
        j, k = at
        ref, n = self.place(j)
        return ref[n, self.first + k]

    def place(self, j):
        west_part, own, east_part = self.parts
        if j < 0:
            return west_part, max(j + HALO, 0)
        if j < GROUP:
            return own, j
        return east_part, min(j - GROUP, HALO - 1)

    def put(self, j, k, value):
        ref, n = self.place(j)
        ref[n, k] = value


def tangent_step(levels, sel, coupling, src, winds, step, tiles, emit):
    @pl.loop(0, levels)
    def _(lv):
        for j in tiles:
            u = winds[j, 2 * step * levels + lv]
            v = winds[j, (2 * step + 1) * levels + lv]
            f = [src[j, a * levels + lv] for a in range(VARS)]
            for a in range(VARS):
                k = a * levels + lv
                dx = east(sel, f[a], src[j + TY, k]) - west(sel, f[a], src[j - TY, k])
                dy = north(sel, f[a], src[j + 1, k]) - south(sel, f[a], src[j - 1, k])
                emit(j, k, (f[a] + mixed(coupling, f, a, False)) + (u * dx + v * dy))


def adjoint_step(levels, sel, coupling, src, winds, step, tiles, emit):
    @pl.loop(0, levels)
    def _(lv):
        ku = 2 * step * levels + lv
        kv = (2 * step + 1) * levels + lv
        for j in tiles:
            ue = east(sel, winds[j, ku], winds[j + TY, ku])
            uw = west(sel, winds[j, ku], winds[j - TY, ku])
            vn = north(sel, winds[j, kv], winds[j + 1, kv])
            vs = south(sel, winds[j, kv], winds[j - 1, kv])
            g = [src[j, a * levels + lv] for a in range(VARS)]
            for a in range(VARS):
                k = a * levels + lv
                flux = uw * west(sel, g[a], src[j - TY, k]) - ue * east(sel, g[a], src[j + TY, k])
                flux += vs * south(sel, g[a], src[j - 1, k]) - vn * north(sel, g[a], src[j + 1, k])
                emit(j, k, (g[a] + mixed(coupling, g, a, True)) + flux)


def precision_step(levels, sel, prec, src, tiles, emit):
    @pl.loop(0, levels)
    def _(lv):
        for j in tiles:
            for a in range(VARS):
                k = a * levels + lv
                f = src[j, k]
                around = east(sel, f, src[j + TY, k]) + west(sel, f, src[j - TY, k])
                around += north(sel, f, src[j + 1, k]) + south(sel, f, src[j - 1, k])
                emit(j, k, prec[a, lv] * ((1.0 + 4.0 * smooth_weight) * f - smooth_weight * around))


OWN = range(GROUP)
WEST, EAST = range(-HALO, 0), range(GROUP, GROUP + HALO)
ALL = range(-HALO, GROUP + HALO)


def put_in(ref):
    def emit(j, k, value):
        ref[j, k] = value

    return emit


def forward_kernel(levels, window, coupling, prec, west_in, own_in, east_in, *refs):
    sel = masks()
    parts = (west_in, own_in, east_in)
    state, winds = Slab(parts), Slab(parts, VARS * levels)
    moved, weighed, f0, f1 = Slab(refs[:3]), refs[3], Slab(refs[4:7]), Slab(refs[7:10])

    @pl.when(window[0] != window[1])
    def _():
        tangent_step(levels, sel, coupling, state, winds, 0, ALL, f0.put)
        tangent_step(levels, sel, coupling, f0, winds, 1, ALL, f1.put)
        tangent_step(levels, sel, coupling, f1, winds, 2, ALL, moved.put)
        precision_step(levels, sel, prec, moved, OWN, put_in(weighed))


def backward_kernel(levels, window, coupling, prec, follow_own, follow_halo, *refs):
    sel = masks()
    moved, parts, out = Slab(refs[:3]), refs[3:6], refs[6]
    f0, f1 = Slab(refs[7:10]), Slab(refs[10:13])
    state, winds = Slab(parts), Slab(parts, VARS * levels)
    follow = Slab((follow_halo.at[pl.ds(0, HALO)], follow_own, follow_halo.at[pl.ds(HALO, HALO)]))

    precision_step(levels, sel, prec, state, OWN, put_in(out))

    @pl.when(window[0] != window[1])
    def _():
        def result(j, k, value):
            out[j, k] = out[j, k] - value

        @pl.loop(0, VARS * levels)
        def _(k):
            for j in ALL:
                f1.put(j, k, follow[j, k] - moved[j, k])

        precision_step(levels, sel, prec, f1, ALL, f0.put)
        adjoint_step(levels, sel, coupling, f0, winds, 2, ALL, f1.put)
        adjoint_step(levels, sel, coupling, f1, winds, 1, ALL[1:-1], f0.put)
        adjoint_step(levels, sel, coupling, f0, winds, 0, OWN, result)


def with_halo(x):
    return shifted(x[GROUP - HALO :], "tile", GROUP), x, shifted(x[:HALO], "tile", -GROUP)


def body(state, obs_weight, trajectory, coupling, prec_scale):
    own_state = state[0, 0]
    levels = own_state.shape[1] // GROUP
    cell = own_state.shape[2:]
    winds = trajectory[0, 0].reshape((2 * STEPS,) + own_state.shape[1:]).astype(jnp.float32)
    fields = VARS * levels
    window_index = lax.axis_index("win")
    last_window = lax.axis_size("win") - 1
    window = jnp.stack([window_index, jnp.int32(last_window)]).astype(jnp.int32)
    prec = lax.dynamic_slice_in_dim(prec_scale, (lax.axis_index("tile") % GROUP) * levels, levels, axis=1)

    def by_level(x):
        kinds = x.shape[0]
        x = x.reshape((kinds, GROUP, levels) + cell)
        return jnp.moveaxis(x, 1, 0).reshape((GROUP, kinds * levels) + cell)

    slab = exchange(by_level(jnp.concatenate([own_state, winds])))
    parts = with_halo(slab)
    follow_own = passed_along(slab[:, :fields], "win", -1)
    follow_halo = passed_along(jnp.concatenate([parts[0][:, :fields], parts[2][:, :fields]]), "win", -1)

    smem = pl.BlockSpec(memory_space=pltpu.SMEM)
    vmem = pl.BlockSpec(memory_space=pltpu.VMEM)
    core_shape = jax.ShapeDtypeStruct((GROUP, fields) + cell, jnp.float32)
    halo_shape = jax.ShapeDtypeStruct((HALO, fields) + cell, jnp.float32)
    slab_shapes = (halo_shape, core_shape, halo_shape)
    slab_scratch = [pltpu.VMEM(x.shape, x.dtype) for x in slab_shapes]
    params = pltpu.CompilerParams(vmem_limit_bytes=12 * 2**20)

    def cost(flops, moved_bytes):
        return pl.CostEstimate(flops=flops, bytes_accessed=moved_bytes, transcendentals=0)

    *moved, weighed = pl.pallas_call(
        functools.partial(forward_kernel, levels),
        out_shape=slab_shapes + (core_shape,),
        in_specs=[smem] * 3 + [vmem] * 3,
        out_specs=(vmem,) * 4,
        scratch_shapes=slab_scratch * 2,
        compiler_params=params,
        cost_estimate=cost(10_000_000, 12_000_000),
        name="forward",
    )(window, coupling, prec, *parts)
    earlier = passed_along(weighed, "win", 1)
    partial = pl.pallas_call(
        functools.partial(backward_kernel, levels),
        out_shape=core_shape,
        in_specs=[smem] * 3 + [vmem] * 8,
        out_specs=vmem,
        scratch_shapes=slab_scratch * 2,
        compiler_params=params,
        cost_estimate=cost(12_000_000, 14_000_000),
        name="backward",
    )(window, coupling, prec, follow_own, follow_halo, *moved, *parts)
    back = exchange(partial - earlier)
    back = jnp.moveaxis(back.reshape((GROUP, VARS, levels) + cell), 0, 1).reshape(own_state.shape)
    return (back + obs_weight[0, 0] * own_state)[None, None]


def solution(mesh):
    in_specs = (
        P("win", "tile", None, None, None, None),
        P("win", "tile", None, None, None, None),
        P("win", "tile", None, None, None, None, None),
        P(),
        P(),
    )
    out_specs = P("win", "tile", None, None, None, None)
    return jax.shard_map(body, mesh=mesh, in_specs=in_specs, out_specs=out_specs, check_vma=False)
```

profile of v0, /device:TPU:1, one launch (start us, length us, event | category | flops | bytes accessed | tf_op | source)
XLA Modules:
  0.0 107.5 jit_solution(4985559981397081676)
XLA Ops:
  0.0 1.1 %convert.1 = f32[6,16,2,8,128]{4,3,2,1,0:T(8,128)S(1)} convert(bf16[6,16,2,8,128]{4,3,2,1,0:T(8,128)(2,1)} %bitcast.15) | non-fusion elementwise | flops 196608 | bytes 1179648 | tf_op jit(solution)/shard_map/convert_element_type | solution.py:186
  1.1 0.1 copy-done.2
  1.2 0.1 pad_maximum_fusion
  1.3 0.1 copy.9
  1.4 46.2 %all_to_all.10.own_in.refs_4_ = f32[16,22,8,128]{3,2,1,0:T(8,128)S(1)} all-to-all(f32[16,22,8,128]{3,2,1,0:T(8,128)S(1)} %bitcast.11), channel_id=1, replica_groups={{0,1,2,3,4,5,6,7,8,9,10,11,12,13,14,15},{16,17,18,19,20,21,22,23,24,25,..., dimensions={0} | all-to-all | bytes 2883584 | tf_op jit(solution)/shard_map/all_to_all | solution.py:31
  47.7 0.8 fusion
  48.5 1.2 %collective-permute-start.1 = (f32[5,22,8,128]{3,2,1,0:T(8,128)}, f32[5,22,8,128]{3,2,1,0:T(8,128)S(1)}, u32[]{:S(2)}, u32[]{:S(2)}) collective-permute-start(f32[5,22,8,128]{3,2,1,0:T(8,128)} %get-tuple-element.13), channel_id=1, source_target_pairs={{0,16},{1,17},{2,18},{3,19},{4,20},{5,21},{6,22},{7,23},{8,24},{9,... | collective-permute-start | bytes 1351688 | tf_op jit(solution)/shard_map/ppermute | solution.py:26
  49.7 1.5 %collective-permute-start.2 = (f32[5,22,8,128]{3,2,1,0:T(8,128)S(1)}, f32[5,22,8,128]{3,2,1,0:T(8,128)S(1)}, u32[]{:S(2)}, u32[]{:S(2)}) collective-permute-start(f32[5,22,8,128]{3,2,1,0:T(8,128)S(1)} %get-tuple-element.14), channel_id=1, source_target_pairs={{0,48},{1,49},{2,50},{3,51},{4,52},{5,53},{6,54},{7,55},{8,56},{9,... | collective-permute-start | bytes 1351688 | tf_op jit(solution)/shard_map/ppermute | solution.py:26
  51.2 0.1 constant_dynamic-slice_fusion.prec
  51.3 5.3 %collective-permute-start = (f32[16,10,8,128]{3,2,1,0:T(8,128)S(1)}, f32[16,10,8,128]{3,2,1,0:T(8,128)S(1)}, u32[]{:S(2)}, u32[]{:S(2)}) collective-permute-start(f32[16,10,8,128]{3,2,1,0:T(8,128)S(1)} %slice.20), channel_id=1, source_target_pairs={{64,0},{128,64},{192,128},{65,1},{129,65},{193,129},{66,2},{130,66... | collective-permute-start | bytes 1966088 | tf_op jit(solution)/shard_map/ppermute | solution.py:21
  56.6 0.1 pad_add_fusion.window
  56.7 2.3 %collective-permute-done.1.west_in.refs_3_ = f32[5,22,8,128]{3,2,1,0:T(8,128)S(1)} collective-permute-done((f32[5,22,8,128]{3,2,1,0:T(8,128)}, f32[5,22,8,128]{3,2,1,0:T(8,128)S(1)}, u32[]{:S(2)}, u32[]{:S(2)}) %collective-permute-start.1) | collective-permute-done | bytes 450592 | tf_op jit(solution)/shard_map/ppermute | solution.py:26
  58.9 0.0 collective-permute-done.2.east_in.refs_5_
  58.9 3.9 %forward.1 = (f32[5,10,8,128]{3,2,1,0:T(8,128)S(1)}, f32[16,10,8,128]{3,2,1,0:T(8,128)S(1)}, f32[5,10,8,128]{3,2,1,0:T(8,128)S(1)}, f32[16,10,8,128]{3,2,1,0:T(8,128)S(1)}) custom-call(s32[2]{0:T(128)S(1)} %pad_add_fusion.window, f32[5,5]{1,0:T(8,128)S(1)} %copy-done.1, f32[5,2]{1,0:T(8,128)S(1)} %constant_dynamic-slice_fusion.prec, ...), custom_call_target="tpu_custom_call" | custom-call | flops 10000000 | bytes 12000000 | tf_op jit(solution)/shard_map/forward/pallas_call | solution.py:214
  62.8 5.9 %collective-permute-start.4 = (f32[16,10,8,128]{3,2,1,0:T(8,128)S(1)}, f32[16,10,8,128]{3,2,1,0:T(8,128)S(1)}, u32[]{:S(2)}, u32[]{:S(2)}) collective-permute-start(f32[16,10,8,128]{3,2,1,0:T(8,128)S(1)} %get-tuple-element.12), channel_id=1, source_target_pairs={{0,64},{64,128},{128,192},{1,65},{65,129},{129,193},{2,66},{66,130... | collective-permute-start | bytes 1966088 | tf_op jit(solution)/shard_map/ppermute | solution.py:21
  68.8 1.9 %collective-permute-start.3 = (f32[10,10,8,128]{3,2,1,0:T(8,128)S(1)}, f32[10,10,8,128]{3,2,1,0:T(8,128)S(1)}, u32[]{:S(2)}, u32[]{:S(2)}) collective-permute-start(f32[10,10,8,128]{3,2,1,0:T(8,128)S(1)} %pad_maximum_fusion.1), channel_id=1, source_target_pairs={{64,0},{128,64},{192,128},{65,1},{129,65},{193,129},{66,2},{130,66... | collective-permute-start | bytes 1228808 | tf_op jit(solution)/shard_map/ppermute | solution.py:21
  70.8 0.0 collective-permute-done.follow_own
  70.8 7.3 %collective-permute-done.3.follow_halo = f32[10,10,8,128]{3,2,1,0:T(8,128)S(1)} collective-permute-done((f32[10,10,8,128]{3,2,1,0:T(8,128)S(1)}, f32[10,10,8,128]{3,2,1,0:T(8,128)S(1)}, u32[]{:S(2)}, u32[]{:S(2)}) %collective-permute-start.3) | collective-permute-done | bytes 409632 | tf_op jit(solution)/shard_map/ppermute | solution.py:21
  78.1 4.8 %backward.1 = f32[16,10,8,128]{3,2,1,0:T(8,128)S(1)} custom-call(s32[2]{0:T(128)S(1)} %pad_add_fusion.window, f32[5,5]{1,0:T(8,128)S(1)} %copy-done.1, f32[5,2]{1,0:T(8,128)S(1)} %constant_dynamic-slice_fusion.prec, f32[16,10,8,128]{3,2,1,0:T(8,128)S(1)} %collective-permute-done.follow_own, f32[10,10,8,128]{3,2,1,0:T(8,128)S(1)} %collective-permute-done.3.follow_halo, ...), custom_call_target="tpu_custom_call" | custom-call | flops 12000000 | bytes 14000000 | tf_op jit(solution)/shard_map/backward/pallas_call | solution.py:225
  82.9 0.0 collective-permute-done.4
  82.9 0.1 sub.3
  83.0 0.0 copy-start.3
  83.0 23.5 %all_to_all.11 = f32[16,10,8,128]{3,2,1,0:T(8,128)S(1)} all-to-all(f32[16,10,8,128]{3,2,1,0:T(8,128)S(1)} %sub.3), channel_id=1, replica_groups={{0,1,2,3,4,5,6,7,8,9,10,11,12,13,14,15},{16,17,18,19,20,21,22,23,24,25,..., dimensions={0} | all-to-all | bytes 1310720 | tf_op jit(solution)/shard_map/all_to_all | solution.py:31
  106.5 1.0 multiply_add_fusion
  (11 shorter events, 0.2 us)
Async XLA Ops:
  0.0 51.2 %copy-start = (f32[5,32]{1,0:T(8,128)S(1)}, f32[5,32]{1,0:T(8,128)}, u32[]{:S(2)}) copy-start(f32[5,32]{1,0:T(8,128)} %param.9) | copy-start | bytes 1924
  0.0 1.2 %copy-start.2 = (f32[1,1,5,32,8,128]{5,4,3,2,1,0:T(8,128)S(1)}, f32[1,1,5,32,8,128]{5,4,3,2,1,0:T(8,128)}, u32[]{:S(2)}) copy-start(f32[1,1,5,32,8,128]{5,4,3,2,1,0:T(8,128)} %param.5) | copy-start | bytes 1966084
  47.7 11.3 %copy-start.1 = (f32[5,5]{1,0:T(8,128)S(1)}, f32[5,5]{1,0:T(8,128)}, u32[]{:S(2)}) copy-start(f32[5,5]{1,0:T(8,128)} %coupling.3) | copy-start | bytes 304
  48.5 10.4 %collective-permute-start.1 = (f32[5,22,8,128]{3,2,1,0:T(8,128)}, f32[5,22,8,128]{3,2,1,0:T(8,128)S(1)}, u32[]{:S(2)}, u32[]{:S(2)}) collective-permute-start(f32[5,22,8,128]{3,2,1,0:T(8,128)} %get-tuple-element.13), channel_id=1, source_target_pairs={{0,16},{1,17},{2,18},{3,19},{4,20},{5,21},{6,22},{7,23},{8,24},{9,... | collective-permute-start | bytes 1351688 | tf_op jit(solution)/shard_map/ppermute | solution.py:26
  49.7 9.2 %collective-permute-start.2 = (f32[5,22,8,128]{3,2,1,0:T(8,128)S(1)}, f32[5,22,8,128]{3,2,1,0:T(8,128)S(1)}, u32[]{:S(2)}, u32[]{:S(2)}) collective-permute-start(f32[5,22,8,128]{3,2,1,0:T(8,128)S(1)} %get-tuple-element.14), channel_id=1, source_target_pairs={{0,48},{1,49},{2,50},{3,51},{4,52},{5,53},{6,54},{7,55},{8,56},{9,... | collective-permute-start | bytes 1351688 | tf_op jit(solution)/shard_map/ppermute | solution.py:26
  51.3 19.5 %collective-permute-start = (f32[16,10,8,128]{3,2,1,0:T(8,128)S(1)}, f32[16,10,8,128]{3,2,1,0:T(8,128)S(1)}, u32[]{:S(2)}, u32[]{:S(2)}) collective-permute-start(f32[16,10,8,128]{3,2,1,0:T(8,128)S(1)} %slice.20), channel_id=1, source_target_pairs={{64,0},{128,64},{192,128},{65,1},{129,65},{193,129},{66,2},{130,66... | collective-permute-start | bytes 1966088 | tf_op jit(solution)/shard_map/ppermute | solution.py:21
  62.8 20.1 %collective-permute-start.4 = (f32[16,10,8,128]{3,2,1,0:T(8,128)S(1)}, f32[16,10,8,128]{3,2,1,0:T(8,128)S(1)}, u32[]{:S(2)}, u32[]{:S(2)}) collective-permute-start(f32[16,10,8,128]{3,2,1,0:T(8,128)S(1)} %get-tuple-element.12), channel_id=1, source_target_pairs={{0,64},{64,128},{128,192},{1,65},{65,129},{129,193},{2,66},{66,130... | collective-permute-start | bytes 1966088 | tf_op jit(solution)/shard_map/ppermute | solution.py:21
  68.8 9.3 %collective-permute-start.3 = (f32[10,10,8,128]{3,2,1,0:T(8,128)S(1)}, f32[10,10,8,128]{3,2,1,0:T(8,128)S(1)}, u32[]{:S(2)}, u32[]{:S(2)}) collective-permute-start(f32[10,10,8,128]{3,2,1,0:T(8,128)S(1)} %pad_maximum_fusion.1), channel_id=1, source_target_pairs={{64,0},{128,64},{192,128},{65,1},{129,65},{193,129},{66,2},{130,66... | collective-permute-start | bytes 1228808 | tf_op jit(solution)/shard_map/ppermute | solution.py:21
  83.0 23.6 %copy-start.3 = (f32[1,1,5,32,8,128]{5,4,3,2,1,0:T(8,128)S(1)}, f32[1,1,5,32,8,128]{5,4,3,2,1,0:T(8,128)}, u32[]{:S(2)}) copy-start(f32[1,1,5,32,8,128]{5,4,3,2,1,0:T(8,128)} %param.6) | copy-start | bytes 1966084
where the time goes:
time: 108 us
  blocking collectives  69.7 us (65%)
  starting transfers between devices  15.8 us (15%)
  waiting for transfers between devices  9.61 us (9%)
  Pallas kernels  8.63 us (8%)
  other arithmetic  2.43 us (2%)
  local copies, waits for them, and re-layouts  1.21 us (1%)
    all_to_all x2, blocking collectives, exchange(): return lax.all_to_all(x, 'tile', 0, 0, axis_index_groups=groups, tiled=True)  69.7 us
    ppermute x3, starting transfers between devices, passed_along(): return lax.ppermute(x, axis, pairs)  13.1 us
    ppermute x3, waiting for transfers between devices, passed_along(): return lax.ppermute(x, axis, pairs)  7.34 us
    pallas_call x1, Pallas kernels, body(): pl.pallas_call(functools.partial(backward_kernel, levels), out_shape=core...  4.75 us
    pallas_call x1, Pallas kernels, body(): pl.pallas_call(functools.partial(forward_kernel, levels), out_shape=slab_...  3.88 us
    ppermute x2, starting transfers between devices, shifted(): lax.ppermute(x, axis, [(i, (i + by) % devices) for i in range(devices)])  2.68 us
    ppermute x2, waiting for transfers between devices, shifted(): lax.ppermute(x, axis, [(i, (i + by) % devices) for i in range(devices)])  2.27 us
  transfers between devices with their start and end apart: 5, of which 2 were waited for; matrix products, arithmetic and copies ran while one was open for 0% of the time, Pallas kernels for 8%

commit v1 on v0

--- a/solution.py
+++ b/solution.py
@@ -10,8 +10,9 @@
 VARS = 5
 STEPS = 3
 GROUP = 16
-HALO = 5
 TY = 4
+HALO = TY + 1
+CORNER = 8
 smooth_weight = 0.2
 
 
@@ -78,6 +79,24 @@
     def put(self, j, k, value):
         ref, n = self.place(j)
         ref[n, k] = value
+
+
+class Received:
+    def __init__(self, west_packed, west_corner, own, east_packed, east_corner, first=0):
+        self.west, self.east = (west_packed, west_corner), (east_packed, east_corner)
+        self.own, self.first, self.planes = own, first, own.shape[1]
+
+    def __getitem__(self, at):
+        j, k = at[0], self.first + at[1]
+        if j < -TY:
+            return self.west[1][k]
+        if j < 0:
+            return self.west[0][(j + TY) * self.planes + k]
+        if j < GROUP:
+            return self.own[j, k]
+        if j < GROUP + TY:
+            return self.east[0][(j - GROUP) * self.planes + k]
+        return self.east[1][k]
 
 
 def tangent_step(levels, sel, coupling, src, winds, step, tiles, emit):
@@ -136,11 +155,66 @@
     return emit
 
 
+SLOTS = 128 // CORNER
+
+
+def pack_corner(tile, out, at, shift):
+    slot = lax.broadcasted_iota(jnp.int32, (8, 128), 1) // CORNER
+    for first in range(0, len(tile), SLOTS):
+        packed = jnp.zeros((8, 128), jnp.float32)
+        for q, plane in enumerate(tile[first : first + SLOTS]):
+            packed = jnp.where(slot == q, pltpu.roll(plane, (CORNER * q + shift) % 128, 1), packed)
+        out[at + first // SLOTS] = packed
+
+
+def unpack_corner(packed, at, out, shift):
+    for k in range(out.shape[0]):
+        out[k] = pltpu.roll(packed[at + k // SLOTS], (-CORNER * (k % SLOTS) - shift) % 128, 1)
+
+
+def pack_kernel(fields, own, east_going, west_going, follow_east_going, follow_west_going):
+    top = lax.broadcasted_iota(jnp.int32, (8, 128), 0) < 4
+    count = own.shape[1]
+    half = fields // 2
+    for out, follow_out, first, paired, whole, corner, shift in (
+        (east_going, follow_east_going, GROUP - TY, GROUP - TY, GROUP - 1, GROUP - HALO, CORNER),
+        (west_going, follow_west_going, 0, 1, 0, TY, 0),
+    ):
+        for n in range(TY):
+            out[pl.ds(n * count, count)] = own[first + n]
+        follow_out[pl.ds((TY - 1) * half, fields)] = own[whole, pl.ds(0, fields)]
+        for n in range(TY - 1):
+            for k in range(0, fields, 2):
+                one, two = own[paired + n, k], own[paired + n, k + 1]
+                if shift:
+                    pair = jnp.where(top, pltpu.roll(one, 4, 0), two)
+                else:
+                    pair = jnp.where(top, one, pltpu.roll(two, 4, 0))
+                follow_out[n * half + k // 2] = pair
+        tile = [own[corner, k] for k in range(count)]
+        pack_corner(tile, out, TY * count, shift)
+        pack_corner(tile[:fields], follow_out, (TY + 1) * half, shift)
+
+
+def put_in(ref):
+    def emit(j, k, value):
+        ref[j, k] = value
+
+    return emit
+
+
+def received(west_in, own_in, east_in, west_corner, east_corner, first):
+    at = TY * own_in.shape[1]
+    unpack_corner(west_in, at, west_corner, CORNER)
+    unpack_corner(east_in, at, east_corner, 0)
+    return [Received(west_in, west_corner, own_in, east_in, east_corner, f) for f in (0, first)]
+
+
 def forward_kernel(levels, window, coupling, prec, west_in, own_in, east_in, *refs):
+    refs = refs[2:]
     sel = masks()
-    parts = (west_in, own_in, east_in)
-    state, winds = Slab(parts), Slab(parts, VARS * levels)
     moved, weighed, f0, f1 = Slab(refs[:3]), refs[3], Slab(refs[4:7]), Slab(refs[7:10])
+    state, winds = received(west_in, own_in, east_in, *refs[10:12], VARS * levels)
 
     @pl.when(window[0] != window[1])
     def _():
@@ -150,12 +224,12 @@
         precision_step(levels, sel, prec, moved, OWN, put_in(weighed))
 
 
-def backward_kernel(levels, window, coupling, prec, follow_own, follow_halo, *refs):
+def backward_kernel(levels, window, coupling, prec, follow_west, follow_own, follow_east, *refs):
     sel = masks()
-    moved, parts, out = Slab(refs[:3]), refs[3:6], refs[6]
+    moved, out = Slab(refs[:3]), refs[6]
     f0, f1 = Slab(refs[7:10]), Slab(refs[10:13])
-    state, winds = Slab(parts), Slab(parts, VARS * levels)
-    follow = Slab((follow_halo.at[pl.ds(0, HALO)], follow_own, follow_halo.at[pl.ds(HALO, HALO)]))
+    state, winds = received(*refs[3:6], *refs[13:15], VARS * levels)
+    fields = VARS * levels
 
     precision_step(levels, sel, prec, state, OWN, put_in(out))
 
@@ -164,10 +238,26 @@
         def result(j, k, value):
             out[j, k] = out[j, k] - value
 
-        @pl.loop(0, VARS * levels)
+        half = fields // 2
+        for k in range(fields):
+            for n in range(TY - 1):
+                west_pair, east_pair = follow_west[n * half + k // 2], follow_east[n * half + k // 2]
+                if k % 2 == 0:
+                    west_pair = pltpu.roll(west_pair, 4, 0)
+                else:
+                    east_pair = pltpu.roll(east_pair, 4, 0)
+                f1.put(n - TY, k, west_pair - moved[n - TY, k])
+                f1.put(GROUP + 1 + n, k, east_pair - moved[GROUP + 1 + n, k])
+            f1.put(-1, k, follow_west[(TY - 1) * half + k] - moved[-1, k])
+            f1.put(GROUP, k, follow_east[(TY - 1) * half + k] - moved[GROUP, k])
+            at, turn = (TY + 1) * half + k // SLOTS, CORNER * (k % SLOTS)
+            f1.put(-HALO, k, pltpu.roll(follow_west[at], (-turn - CORNER) % 128, 1) - moved[-HALO, k])
+            f1.put(GROUP + TY, k, pltpu.roll(follow_east[at], -turn % 128, 1) - moved[GROUP + TY, k])
+
+        @pl.loop(0, fields)
         def _(k):
-            for j in ALL:
-                f1.put(j, k, follow[j, k] - moved[j, k])
+            for j in OWN:
+                f1.put(j, k, follow_own[j, k] - moved[j, k])
 
         precision_step(levels, sel, prec, f1, ALL, f0.put)
         adjoint_step(levels, sel, coupling, f0, winds, 2, ALL, f1.put)
@@ -175,8 +265,10 @@
         adjoint_step(levels, sel, coupling, f0, winds, 0, OWN, result)
 
 
-def with_halo(x):
-    return shifted(x[GROUP - HALO :], "tile", GROUP), x, shifted(x[:HALO], "tile", -GROUP)
+def from_following(x, by):
+    windows, tiles = lax.axis_size("win"), lax.axis_size("tile")
+    pairs = [(w * tiles + t, (w - 1) * tiles + (t + by) % tiles) for w in range(1, windows) for t in range(tiles)]
+    return lax.ppermute(x, ("win", "tile"), pairs)
 
 
 def body(state, obs_weight, trajectory, coupling, prec_scale):
@@ -196,10 +288,6 @@
         return jnp.moveaxis(x, 1, 0).reshape((GROUP, kinds * levels) + cell)
 
     slab = exchange(by_level(jnp.concatenate([own_state, winds])))
-    parts = with_halo(slab)
-    follow_own = passed_along(slab[:, :fields], "win", -1)
-    follow_halo = passed_along(jnp.concatenate([parts[0][:, :fields], parts[2][:, :fields]]), "win", -1)
-
     smem = pl.BlockSpec(memory_space=pltpu.SMEM)
     vmem = pl.BlockSpec(memory_space=pltpu.VMEM)
     core_shape = jax.ShapeDtypeStruct((GROUP, fields) + cell, jnp.float32)
@@ -211,27 +299,48 @@
     def cost(flops, moved_bytes):
         return pl.CostEstimate(flops=flops, bytes_accessed=moved_bytes, transcendentals=0)
 
+    def flat(n):
+        return jax.ShapeDtypeStruct((n,) + cell, jnp.float32)
+
+    count = slab.shape[1]
+    packed = flat(TY * count + pl.cdiv(count, SLOTS))
+    follow_packed = flat((TY + 1) * (fields // 2) + pl.cdiv(fields, SLOTS))
+    east_going, west_going, follow_east_going, follow_west_going = pl.pallas_call(
+        functools.partial(pack_kernel, fields),
+        out_shape=(packed, packed, follow_packed, follow_packed),
+        in_specs=[vmem],
+        out_specs=(vmem,) * 4,
+        compiler_params=params,
+        name="pack",
+    )(slab)
+    parts = (shifted(east_going, "tile", GROUP), slab, shifted(west_going, "tile", -GROUP))
+    follow_parts = (
+        from_following(follow_east_going, GROUP),
+        passed_along(slab[:, :fields], "win", -1),
+        from_following(follow_west_going, -GROUP),
+    )
+    corner = pltpu.VMEM((count,) + cell, jnp.float32)
     *moved, weighed = pl.pallas_call(
         functools.partial(forward_kernel, levels),
         out_shape=slab_shapes + (core_shape,),
-        in_specs=[smem] * 3 + [vmem] * 3,
+        in_specs=[smem] * 3 + [vmem] * 3 + [pl.BlockSpec(memory_space=pl.ANY)] * 2,
         out_specs=(vmem,) * 4,
-        scratch_shapes=slab_scratch * 2,
+        scratch_shapes=slab_scratch * 2 + [corner] * 2,
         compiler_params=params,
         cost_estimate=cost(10_000_000, 12_000_000),
         name="forward",
-    )(window, coupling, prec, *parts)
+    )(window, coupling, prec, *parts, follow_parts[0], follow_parts[2])
     earlier = passed_along(weighed, "win", 1)
     partial = pl.pallas_call(
         functools.partial(backward_kernel, levels),
         out_shape=core_shape,
-        in_specs=[smem] * 3 + [vmem] * 8,
+        in_specs=[smem] * 3 + [vmem] * 9,
         out_specs=vmem,
-        scratch_shapes=slab_scratch * 2,
+        scratch_shapes=slab_scratch * 2 + [corner] * 2,
         compiler_params=params,
         cost_estimate=cost(12_000_000, 14_000_000),
         name="backward",
-    )(window, coupling, prec, follow_own, follow_halo, *moved, *parts)
+    )(window, coupling, prec, *follow_parts, *moved, *parts)
     back = exchange(partial - earlier)
     back = jnp.moveaxis(back.reshape((GROUP, VARS, levels) + cell), 0, 1).reshape(own_state.shape)
     return (back + obs_weight[0, 0] * own_state)[None, None]

time: 108 us -> 105 us (0.972)
  starting transfers between devices: 15.8 us -> 14.3 us
  waiting for transfers between devices: 9.61 us -> 8.4 us
    ppermute x0 -> x2, waiting for transfers between devices: none -> 5.79 us  [from_following(): return lax.ppermute(x, ('win', 'tile'), pairs)]
    ppermute x3 -> x2, starting transfers between devices: 13.1 us -> 7.71 us  [passed_along(): return lax.ppermute(x, axis, pairs)]
    ppermute x3 -> x2, waiting for transfers between devices: 7.34 us -> 2.61 us  [passed_along(): return lax.ppermute(x, axis, pairs)]
    ppermute x0 -> x2, starting transfers between devices: none -> 3.84 us  [from_following(): return lax.ppermute(x, ('win', 'tile'), pairs)]
    ppermute x2, waiting for transfers between devices: 2.27 us -> 0.01 us  [shifted(): lax.ppermute(x, axis, [(i, (i + by) % devices) for i in range(devices)])]
  transfers between devices with their start and end apart: 5 -> 6, of which waited for: 2 -> 3; matrix products, arithmetic and copies ran while one was open for 0% -> 0% of each run, Pallas kernels for 8% -> 8%
where the time goes in v1:
time: 105 us
  blocking collectives  70.6 us (67%)
  starting transfers between devices  14.3 us (14%)
  Pallas kernels  8.99 us (9%)
  waiting for transfers between devices  8.4 us (8%)
  other arithmetic  2.3 us (2%)
    all_to_all x2, blocking collectives, exchange(): return lax.all_to_all(x, 'tile', 0, 0, axis_index_groups=groups, tiled=True)  70.6 us
    ppermute x2, starting transfers between devices, passed_along(): return lax.ppermute(x, axis, pairs)  7.71 us
    ppermute x2, waiting for transfers between devices, from_following(): return lax.ppermute(x, ('win', 'tile'), pairs)  5.79 us
    pallas_call x1, Pallas kernels, body(): pl.pallas_call(functools.partial(backward_kernel, levels), out_shape=core...  4.88 us
    pallas_call x1, Pallas kernels, body(): pl.pallas_call(functools.partial(forward_kernel, levels), out_shape=slab_...  3.99 us
    ppermute x2, starting transfers between devices, from_following(): return lax.ppermute(x, ('win', 'tile'), pairs)  3.84 us
    ppermute x2, starting transfers between devices, shifted(): lax.ppermute(x, axis, [(i, (i + by) % devices) for i in range(devices)])  2.75 us
    ppermute x2, waiting for transfers between devices, passed_along(): return lax.ppermute(x, axis, pairs)  2.61 us
  transfers between devices with their start and end apart: 6, of which 3 were waited for; matrix products, arithmetic and copies ran while one was open for 0% of the time, Pallas kernels for 8%

profile of v1, /device:TPU:1, one launch (start us, length us, event | category | flops | bytes accessed | tf_op | source)
XLA Modules:
  0.0 105.0 jit_solution(3853974221781720719)
XLA Ops:
  0.0 1.1 %convert.1 = f32[6,16,2,8,128]{4,3,2,1,0:T(8,128)S(1)} convert(bf16[6,16,2,8,128]{4,3,2,1,0:T(8,128)(2,1)} %bitcast.15) | non-fusion elementwise | flops 196608 | bytes 1179648 | tf_op jit(solution)/shard_map/convert_element_type | solution.py:278
  1.1 0.1 copy-done.2
  1.2 0.1 pad_maximum_fusion
  1.3 0.1 copy.9
  1.4 46.2 %all_to_all.10.own.own_in.refs_4_ = f32[16,22,8,128]{3,2,1,0:T(8,128)S(1)} all-to-all(f32[16,22,8,128]{3,2,1,0:T(8,128)S(1)} %bitcast.11), channel_id=1, replica_groups={{0,1,2,3,4,5,6,7,8,9,10,11,12,13,14,15},{16,17,18,19,20,21,22,23,24,25,..., dimensions={0} | all-to-all | bytes 2883584 | tf_op jit(solution)/shard_map/all_to_all | solution.py:32
  47.7 0.1 pack.1
  47.8 1.3 %collective-permute-start.3 = (f32[90,8,128]{2,1,0:T(8,128)S(1)}, f32[90,8,128]{2,1,0:T(8,128)S(1)}, u32[]{:S(2)}, u32[]{:S(2)}) collective-permute-start(f32[90,8,128]{2,1,0:T(8,128)S(1)} %get-tuple-element.15), channel_id=1, source_target_pairs={{0,16},{1,17},{2,18},{3,19},{4,20},{5,21},{6,22},{7,23},{8,24},{9,... | collective-permute-start | bytes 1105928 | tf_op jit(solution)/shard_map/ppermute | solution.py:27
  49.1 1.5 %collective-permute-start.4 = (f32[90,8,128]{2,1,0:T(8,128)S(1)}, f32[90,8,128]{2,1,0:T(8,128)S(1)}, u32[]{:S(2)}, u32[]{:S(2)}) collective-permute-start(f32[90,8,128]{2,1,0:T(8,128)S(1)} %get-tuple-element.16), channel_id=1, source_target_pairs={{0,48},{1,49},{2,50},{3,51},{4,52},{5,53},{6,54},{7,55},{8,56},{9,... | collective-permute-start | bytes 1105928 | tf_op jit(solution)/shard_map/ppermute | solution.py:27
  50.5 0.1 constant_dynamic-slice_fusion.prec
  50.6 5.3 %collective-permute-start.1 = (f32[16,10,8,128]{3,2,1,0:T(8,128)S(1)}, f32[16,10,8,128]{3,2,1,0:T(8,128)S(1)}, u32[]{:S(2)}, u32[]{:S(2)}) collective-permute-start(f32[16,10,8,128]{3,2,1,0:T(8,128)S(1)} %slice.4), channel_id=1, source_target_pairs={{64,0},{128,64},{192,128},{65,1},{129,65},{193,129},{66,2},{130,66... | collective-permute-start | bytes 1966088 | tf_op jit(solution)/shard_map/ppermute | solution.py:22
  55.9 1.9 %collective-permute-start = (f32[26,8,128]{2,1,0:T(8,128)S(1)}, f32[26,8,128]{2,1,0:T(8,128)S(1)}, u32[]{:S(2)}, u32[]{:S(2)}) collective-permute-start(f32[26,8,128]{2,1,0:T(8,128)S(1)} %get-tuple-element.13), channel_id=1, source_target_pairs={{64,16},{65,17},{66,18},{67,19},{68,20},{69,21},{70,22},{71,23},{7... | collective-permute-start | bytes 319496 | tf_op jit(solution)/shard_map/ppermute | solution.py:271
  57.9 1.9 %collective-permute-start.2 = (f32[26,8,128]{2,1,0:T(8,128)S(1)}, f32[26,8,128]{2,1,0:T(8,128)S(1)}, u32[]{:S(2)}, u32[]{:S(2)}) collective-permute-start(f32[26,8,128]{2,1,0:T(8,128)S(1)} %get-tuple-element.14), channel_id=1, source_target_pairs={{64,48},{65,49},{66,50},{67,51},{68,52},{69,53},{70,54},{71,55},{7... | collective-permute-start | bytes 319496 | tf_op jit(solution)/shard_map/ppermute | solution.py:271
  59.8 0.1 pad_add_fusion.window
  59.9 4.5 %collective-permute-done.refs_0_.follow_west = f32[26,8,128]{2,1,0:T(8,128)S(1)} collective-permute-done((f32[26,8,128]{2,1,0:T(8,128)S(1)}, f32[26,8,128]{2,1,0:T(8,128)S(1)}, u32[]{:S(2)}, u32[]{:S(2)}) %collective-permute-start) | collective-permute-done | bytes 106528 | tf_op jit(solution)/shard_map/ppermute | solution.py:271
  64.4 1.3 %collective-permute-done.2.refs_1_.follow_east = f32[26,8,128]{2,1,0:T(8,128)S(1)} collective-permute-done((f32[26,8,128]{2,1,0:T(8,128)S(1)}, f32[26,8,128]{2,1,0:T(8,128)S(1)}, u32[]{:S(2)}, u32[]{:S(2)}) %collective-permute-start.2) | collective-permute-done | bytes 106528 | tf_op jit(solution)/shard_map/ppermute | solution.py:271
  65.7 4.0 %forward.1 = (f32[5,10,8,128]{3,2,1,0:T(8,128)S(1)}, f32[16,10,8,128]{3,2,1,0:T(8,128)S(1)}, f32[5,10,8,128]{3,2,1,0:T(8,128)S(1)}, f32[16,10,8,128]{3,2,1,0:T(8,128)S(1)}) custom-call(s32[2]{0:T(128)S(1)} %pad_add_fusion.window, f32[5,5]{1,0:T(8,128)S(1)} %copy-done.1, f32[5,2]{1,0:T(8,128)S(1)} %constant_dynamic-slice_fusion.prec, ...), custom_call_target="tpu_custom_call" | custom-call | flops 10000000 | bytes 12000000 | tf_op jit(solution)/shard_map/forward/pallas_call | solution.py:323
  69.7 2.4 %collective-permute-start.5 = (f32[16,10,8,128]{3,2,1,0:T(8,128)S(1)}, f32[16,10,8,128]{3,2,1,0:T(8,128)S(1)}, u32[]{:S(2)}, u32[]{:S(2)}) collective-permute-start(f32[16,10,8,128]{3,2,1,0:T(8,128)S(1)} %get-tuple-element.20), channel_id=1, source_target_pairs={{0,64},{64,128},{128,192},{1,65},{65,129},{129,193},{2,66},{66,130... | collective-permute-start | bytes 1966088 | tf_op jit(solution)/shard_map/ppermute | solution.py:22
  72.1 4.9 %backward.1 = f32[16,10,8,128]{3,2,1,0:T(8,128)S(1)} custom-call(s32[2]{0:T(128)S(1)} %pad_add_fusion.window, f32[5,5]{1,0:T(8,128)S(1)} %copy-done.1, f32[5,2]{1,0:T(8,128)S(1)} %constant_dynamic-slice_fusion.prec, f32[26,8,128]{2,1,0:T(8,128)S(1)} %collective-permute-done.refs_0_.follow_west, f32[16,10,8,128]{3,2,1,0:T(8,128)S(1)} %collective-permute-done.1.follow_own, ...), custom_call_target="tpu_custom_call" | custom-call | flops 12000000 | bytes 14000000 | tf_op jit(solution)/shard_map/backward/pallas_call | solution.py:334
  77.0 2.6 %collective-permute-done.5 = f32[16,10,8,128]{3,2,1,0:T(8,128)S(1)} collective-permute-done((f32[16,10,8,128]{3,2,1,0:T(8,128)S(1)}, f32[16,10,8,128]{3,2,1,0:T(8,128)S(1)}, u32[]{:S(2)}, u32[]{:S(2)}) %collective-permute-start.5) | collective-permute-done | bytes 655392 | tf_op jit(solution)/shard_map/ppermute | solution.py:22
  79.6 0.1 sub.3
  79.7 0.0 copy-start.3
  79.7 0.0 copy-start.4
  79.7 24.3 %all_to_all.11 = f32[16,10,8,128]{3,2,1,0:T(8,128)S(1)} all-to-all(f32[16,10,8,128]{3,2,1,0:T(8,128)S(1)} %sub.3), channel_id=1, replica_groups={{0,1,2,3,4,5,6,7,8,9,10,11,12,13,14,15},{16,17,18,19,20,21,22,23,24,25,..., dimensions={0} | all-to-all | bytes 1310720 | tf_op jit(solution)/shard_map/all_to_all | solution.py:32
  104.1 0.9 multiply_add_fusion
  (12 shorter events, 0.1 us)
Async XLA Ops:
  0.0 50.5 %copy-start = (f32[5,32]{1,0:T(8,128)S(1)}, f32[5,32]{1,0:T(8,128)}, u32[]{:S(2)}) copy-start(f32[5,32]{1,0:T(8,128)} %param.9) | copy-start | bytes 1924
  0.0 1.2 %copy-start.2 = (f32[1,1,5,32,8,128]{5,4,3,2,1,0:T(8,128)S(1)}, f32[1,1,5,32,8,128]{5,4,3,2,1,0:T(8,128)}, u32[]{:S(2)}) copy-start(f32[1,1,5,32,8,128]{5,4,3,2,1,0:T(8,128)} %param.5) | copy-start | bytes 1966084
  47.7 18.0 %copy-start.1 = (f32[5,5]{1,0:T(8,128)S(1)}, f32[5,5]{1,0:T(8,128)}, u32[]{:S(2)}) copy-start(f32[5,5]{1,0:T(8,128)} %coupling.3) | copy-start | bytes 304
  47.8 17.9 %collective-permute-start.3 = (f32[90,8,128]{2,1,0:T(8,128)S(1)}, f32[90,8,128]{2,1,0:T(8,128)S(1)}, u32[]{:S(2)}, u32[]{:S(2)}) collective-permute-start(f32[90,8,128]{2,1,0:T(8,128)S(1)} %get-tuple-element.15), channel_id=1, source_target_pairs={{0,16},{1,17},{2,18},{3,19},{4,20},{5,21},{6,22},{7,23},{8,24},{9,... | collective-permute-start | bytes 1105928 | tf_op jit(solution)/shard_map/ppermute | solution.py:27
  49.1 16.6 %collective-permute-start.4 = (f32[90,8,128]{2,1,0:T(8,128)S(1)}, f32[90,8,128]{2,1,0:T(8,128)S(1)}, u32[]{:S(2)}, u32[]{:S(2)}) collective-permute-start(f32[90,8,128]{2,1,0:T(8,128)S(1)} %get-tuple-element.16), channel_id=1, source_target_pairs={{0,48},{1,49},{2,50},{3,51},{4,52},{5,53},{6,54},{7,55},{8,56},{9,... | collective-permute-start | bytes 1105928 | tf_op jit(solution)/shard_map/ppermute | solution.py:27
  50.6 21.5 %collective-permute-start.1 = (f32[16,10,8,128]{3,2,1,0:T(8,128)S(1)}, f32[16,10,8,128]{3,2,1,0:T(8,128)S(1)}, u32[]{:S(2)}, u32[]{:S(2)}) collective-permute-start(f32[16,10,8,128]{3,2,1,0:T(8,128)S(1)} %slice.4), channel_id=1, source_target_pairs={{64,0},{128,64},{192,128},{65,1},{129,65},{193,129},{66,2},{130,66... | collective-permute-start | bytes 1966088 | tf_op jit(solution)/shard_map/ppermute | solution.py:22
  55.9 8.4 %collective-permute-start = (f32[26,8,128]{2,1,0:T(8,128)S(1)}, f32[26,8,128]{2,1,0:T(8,128)S(1)}, u32[]{:S(2)}, u32[]{:S(2)}) collective-permute-start(f32[26,8,128]{2,1,0:T(8,128)S(1)} %get-tuple-element.13), channel_id=1, source_target_pairs={{64,16},{65,17},{66,18},{67,19},{68,20},{69,21},{70,22},{71,23},{7... | collective-permute-start | bytes 319496 | tf_op jit(solution)/shard_map/ppermute | solution.py:271
  57.9 7.8 %collective-permute-start.2 = (f32[26,8,128]{2,1,0:T(8,128)S(1)}, f32[26,8,128]{2,1,0:T(8,128)S(1)}, u32[]{:S(2)}, u32[]{:S(2)}) collective-permute-start(f32[26,8,128]{2,1,0:T(8,128)S(1)} %get-tuple-element.14), channel_id=1, source_target_pairs={{64,48},{65,49},{66,50},{67,51},{68,52},{69,53},{70,54},{71,55},{7... | collective-permute-start | bytes 319496 | tf_op jit(solution)/shard_map/ppermute | solution.py:271
  69.7 9.9 %collective-permute-start.5 = (f32[16,10,8,128]{3,2,1,0:T(8,128)S(1)}, f32[16,10,8,128]{3,2,1,0:T(8,128)S(1)}, u32[]{:S(2)}, u32[]{:S(2)}) collective-permute-start(f32[16,10,8,128]{3,2,1,0:T(8,128)S(1)} %get-tuple-element.20), channel_id=1, source_target_pairs={{0,64},{64,128},{128,192},{1,65},{65,129},{129,193},{2,66},{66,130... | collective-permute-start | bytes 1966088 | tf_op jit(solution)/shard_map/ppermute | solution.py:22
  79.7 24.4 %copy-start.3 = (f32[1,1,5,32,8,128]{5,4,3,2,1,0:T(8,128)S(1)}, f32[1,1,5,32,8,128]{5,4,3,2,1,0:T(8,128)}, u32[]{:S(2)}) copy-start(f32[1,1,5,32,8,128]{5,4,3,2,1,0:T(8,128)} %param.5) | copy-start | bytes 1966084
  79.7 24.4 %copy-start.4 = (f32[1,1,5,32,8,128]{5,4,3,2,1,0:T(8,128)S(1)}, f32[1,1,5,32,8,128]{5,4,3,2,1,0:T(8,128)}, u32[]{:S(2)}) copy-start(f32[1,1,5,32,8,128]{5,4,3,2,1,0:T(8,128)} %param.6) | copy-start | bytes 1966084

commit v2 on v1

--- a/solution.py
+++ b/solution.py
@@ -211,9 +211,8 @@
 
 
 def forward_kernel(levels, window, coupling, prec, west_in, own_in, east_in, *refs):
-    refs = refs[2:]
     sel = masks()
-    moved, weighed, f0, f1 = Slab(refs[:3]), refs[3], Slab(refs[4:7]), Slab(refs[7:10])
+    moved, own_weighted, f0, f1 = Slab(refs[:3]), refs[3], Slab(refs[4:7]), Slab(refs[7:10])
     state, winds = received(west_in, own_in, east_in, *refs[10:12], VARS * levels)
 
     @pl.when(window[0] != window[1])
@@ -221,22 +220,31 @@
         tangent_step(levels, sel, coupling, state, winds, 0, ALL, f0.put)
         tangent_step(levels, sel, coupling, f0, winds, 1, ALL, f1.put)
         tangent_step(levels, sel, coupling, f1, winds, 2, ALL, moved.put)
-        precision_step(levels, sel, prec, moved, OWN, put_in(weighed))
+
+    precision_step(levels, sel, prec, state, OWN, put_in(own_weighted))
+
+
+def weigh_kernel(levels, window, prec, west_in, own_in, east_in, first, second, weighed):
+    @pl.when(window[0] != window[1])
+    def _():
+        precision_step(levels, masks(), prec, Slab((west_in, own_in, east_in)), OWN, put_in(weighed))
 
 
 def backward_kernel(levels, window, coupling, prec, follow_west, follow_own, follow_east, *refs):
     sel = masks()
-    moved, out = Slab(refs[:3]), refs[6]
-    f0, f1 = Slab(refs[7:10]), Slab(refs[10:13])
-    state, winds = received(*refs[3:6], *refs[13:15], VARS * levels)
+    moved, own_weighted, out = Slab(refs[:3]), refs[3], refs[7]
+    f0, f1 = Slab(refs[8:11]), Slab(refs[11:14])
+    _, winds = received(*refs[4:7], *refs[14:16], VARS * levels)
     fields = VARS * levels
 
-    precision_step(levels, sel, prec, state, OWN, put_in(out))
+    @pl.when(window[0] == window[1])
+    def _():
+        out[...] = own_weighted[...]
 
     @pl.when(window[0] != window[1])
     def _():
         def result(j, k, value):
-            out[j, k] = out[j, k] - value
+            out[j, k] = own_weighted[j, k] - value
 
         half = fields // 2
         for k in range(fields):
@@ -320,27 +328,36 @@
         from_following(follow_west_going, -GROUP),
     )
     corner = pltpu.VMEM((count,) + cell, jnp.float32)
-    *moved, weighed = pl.pallas_call(
+    *moved, own_weighted = pl.pallas_call(
         functools.partial(forward_kernel, levels),
         out_shape=slab_shapes + (core_shape,),
-        in_specs=[smem] * 3 + [vmem] * 3 + [pl.BlockSpec(memory_space=pl.ANY)] * 2,
+        in_specs=[smem] * 3 + [vmem] * 3,
         out_specs=(vmem,) * 4,
         scratch_shapes=slab_scratch * 2 + [corner] * 2,
         compiler_params=params,
         cost_estimate=cost(10_000_000, 12_000_000),
         name="forward",
-    )(window, coupling, prec, *parts, follow_parts[0], follow_parts[2])
+    )(window, coupling, prec, *parts)
+    weighed = pl.pallas_call(
+        functools.partial(weigh_kernel, levels),
+        out_shape=core_shape,
+        in_specs=[smem] * 2 + [vmem] * 3 + [pl.BlockSpec(memory_space=pl.ANY)] * 2,
+        out_specs=vmem,
+        compiler_params=params,
+        cost_estimate=cost(2_000_000, 2_000_000),
+        name="weigh",
+    )(window, prec, *moved, follow_parts[0], follow_parts[2])
     earlier = passed_along(weighed, "win", 1)
     partial = pl.pallas_call(
         functools.partial(backward_kernel, levels),
         out_shape=core_shape,
-        in_specs=[smem] * 3 + [vmem] * 9,
+        in_specs=[smem] * 3 + [vmem] * 10,
         out_specs=vmem,
         scratch_shapes=slab_scratch * 2 + [corner] * 2,
         compiler_params=params,
         cost_estimate=cost(12_000_000, 14_000_000),
         name="backward",
-    )(window, coupling, prec, *follow_parts, *moved, *parts)
+    )(window, coupling, prec, *follow_parts, *moved, own_weighted, *parts)
     back = exchange(partial - earlier)
     back = jnp.moveaxis(back.reshape((GROUP, VARS, levels) + cell), 0, 1).reshape(own_state.shape)
     return (back + obs_weight[0, 0] * own_state)[None, None]

time: 105 us -> 102 us (0.971)
  waiting for transfers between devices: 8.4 us -> 3.11 us
  starting transfers between devices: 14.3 us -> 17.8 us
  blocking collectives: 70.6 us -> 68.4 us
    ppermute x2, waiting for transfers between devices: 5.79 us -> 0.01 us  [from_following(): return lax.ppermute(x, ('win', 'tile'), pairs)]
    ppermute x2, starting transfers between devices: 3.84 us -> 7.72 us  [from_following(): return lax.ppermute(x, ('win', 'tile'), pairs)]
    all_to_all x2, blocking collectives: 70.6 us -> 68.4 us  [exchange(): return lax.all_to_all(x, 'tile', 0, 0, axis_index_groups=groups, tiled=True)]
    pallas_call x0 -> x1, Pallas kernels: none -> 1.1 us  [body(): pl.pallas_call(functools.partial(weigh_kernel, levels), out_shape=core_sh...]
  transfers between devices with their start and end apart: 6 -> 6, of which waited for: 3 -> 2; matrix products, arithmetic and copies ran while one was open for 0% -> 0% of each run, Pallas kernels for 8% -> 9%
where the time goes in v2:
time: 102 us
  blocking collectives  68.4 us (67%)
  starting transfers between devices  17.8 us (17%)
  Pallas kernels  9.61 us (9%)
  waiting for transfers between devices  3.11 us (3%)
  other arithmetic  2.3 us (2%)
    all_to_all x2, blocking collectives, exchange(): return lax.all_to_all(x, 'tile', 0, 0, axis_index_groups=groups, tiled=True)  68.4 us
    ppermute x2, starting transfers between devices, from_following(): return lax.ppermute(x, ('win', 'tile'), pairs)  7.72 us
    ppermute x2, starting transfers between devices, passed_along(): return lax.ppermute(x, axis, pairs)  7.32 us
    pallas_call x1, Pallas kernels, body(): pl.pallas_call(functools.partial(backward_kernel, levels), out_shape=core...  4.4 us
    pallas_call x1, Pallas kernels, body(): pl.pallas_call(functools.partial(forward_kernel, levels), out_shape=slab_...  4 us
    ppermute x2, waiting for transfers between devices, passed_along(): return lax.ppermute(x, axis, pairs)  3.1 us
    ppermute x2, starting transfers between devices, shifted(): lax.ppermute(x, axis, [(i, (i + by) % devices) for i in range(devices)])  2.75 us
  transfers between devices with their start and end apart: 6, of which 2 were waited for; matrix products, arithmetic and copies ran while one was open for 0% of the time, Pallas kernels for 9%

profile of v2, /device:TPU:1, one launch (start us, length us, event | category | flops | bytes accessed | tf_op | source)
XLA Modules:
  0.0 101.7 jit_solution(14271124611570426573)
XLA Ops:
  0.0 1.1 %convert.1 = f32[6,16,2,8,128]{4,3,2,1,0:T(8,128)S(1)} convert(bf16[6,16,2,8,128]{4,3,2,1,0:T(8,128)(2,1)} %bitcast.15) | non-fusion elementwise | flops 196608 | bytes 1179648 | tf_op jit(solution)/shard_map/convert_element_type | solution.py:286
  1.1 0.1 copy-done.2
  1.2 0.1 pad_maximum_fusion
  1.3 0.1 copy.9
  1.4 46.2 %all_to_all.10.own.own_in.refs_5_ = f32[16,22,8,128]{3,2,1,0:T(8,128)S(1)} all-to-all(f32[16,22,8,128]{3,2,1,0:T(8,128)S(1)} %bitcast.11), channel_id=1, replica_groups={{0,1,2,3,4,5,6,7,8,9,10,11,12,13,14,15},{16,17,18,19,20,21,22,23,24,25,..., dimensions={0} | all-to-all | bytes 2883584 | tf_op jit(solution)/shard_map/all_to_all | solution.py:32
  47.7 0.1 pack.1
  47.8 1.3 %collective-permute-start.3 = (f32[90,8,128]{2,1,0:T(8,128)S(1)}, f32[90,8,128]{2,1,0:T(8,128)S(1)}, u32[]{:S(2)}, u32[]{:S(2)}) collective-permute-start(f32[90,8,128]{2,1,0:T(8,128)S(1)} %get-tuple-element.15), channel_id=1, source_target_pairs={{0,16},{1,17},{2,18},{3,19},{4,20},{5,21},{6,22},{7,23},{8,24},{9,... | collective-permute-start | bytes 1105928 | tf_op jit(solution)/shard_map/ppermute | solution.py:27
  49.1 1.5 %collective-permute-start.4 = (f32[90,8,128]{2,1,0:T(8,128)S(1)}, f32[90,8,128]{2,1,0:T(8,128)S(1)}, u32[]{:S(2)}, u32[]{:S(2)}) collective-permute-start(f32[90,8,128]{2,1,0:T(8,128)S(1)} %get-tuple-element.16), channel_id=1, source_target_pairs={{0,48},{1,49},{2,50},{3,51},{4,52},{5,53},{6,54},{7,55},{8,56},{9,... | collective-permute-start | bytes 1105928 | tf_op jit(solution)/shard_map/ppermute | solution.py:27
  50.5 0.1 constant_dynamic-slice_fusion.prec
  50.6 5.2 %collective-permute-start = (f32[26,8,128]{2,1,0:T(8,128)S(1)}, f32[26,8,128]{2,1,0:T(8,128)S(1)}, u32[]{:S(2)}, u32[]{:S(2)}) collective-permute-start(f32[26,8,128]{2,1,0:T(8,128)S(1)} %get-tuple-element.13), channel_id=1, source_target_pairs={{64,16},{65,17},{66,18},{67,19},{68,20},{69,21},{70,22},{71,23},{7... | collective-permute-start | bytes 319496 | tf_op jit(solution)/shard_map/ppermute | solution.py:279
  55.8 2.6 %collective-permute-start.2 = (f32[26,8,128]{2,1,0:T(8,128)S(1)}, f32[26,8,128]{2,1,0:T(8,128)S(1)}, u32[]{:S(2)}, u32[]{:S(2)}) collective-permute-start(f32[26,8,128]{2,1,0:T(8,128)S(1)} %get-tuple-element.14), channel_id=1, source_target_pairs={{64,48},{65,49},{66,50},{67,51},{68,52},{69,53},{70,54},{71,55},{7... | collective-permute-start | bytes 319496 | tf_op jit(solution)/shard_map/ppermute | solution.py:279
  58.3 0.1 pad_add_fusion.window
  58.5 1.9 %collective-permute-start.1 = (f32[16,10,8,128]{3,2,1,0:T(8,128)S(1)}, f32[16,10,8,128]{3,2,1,0:T(8,128)S(1)}, u32[]{:S(2)}, u32[]{:S(2)}) collective-permute-start(f32[16,10,8,128]{3,2,1,0:T(8,128)S(1)} %slice.4), channel_id=1, source_target_pairs={{64,0},{128,64},{192,128},{65,1},{129,65},{193,129},{66,2},{130,66... | collective-permute-start | bytes 1966088 | tf_op jit(solution)/shard_map/ppermute | solution.py:22
  60.4 4.0 %forward.1 = (f32[5,10,8,128]{3,2,1,0:T(8,128)S(1)}, f32[16,10,8,128]{3,2,1,0:T(8,128)S(1)}, f32[5,10,8,128]{3,2,1,0:T(8,128)S(1)}, f32[16,10,8,128]{3,2,1,0:T(8,128)S(1)}) custom-call(s32[2]{0:T(128)S(1)} %pad_add_fusion.window, f32[5,5]{1,0:T(8,128)S(1)} %copy-done.1, f32[5,2]{1,0:T(8,128)S(1)} %constant_dynamic-slice_fusion.prec, ...), custom_call_target="tpu_custom_call" | custom-call | flops 10000000 | bytes 12000000 | tf_op jit(solution)/shard_map/forward/pallas_call | solution.py:331
  64.4 1.1 %weigh.1 = f32[16,10,8,128]{3,2,1,0:T(8,128)S(1)} custom-call(s32[2]{0:T(128)S(1)} %pad_add_fusion.window, f32[5,2]{1,0:T(8,128)S(1)} %constant_dynamic-slice_fusion.prec, f32[5,10,8,128]{3,2,1,0:T(8,128)S(1)} %get-tuple-element.17.refs_0_.west_in, f32[16,10,8,128]{3,2,1,0:T(8,128)S(1)} %get-tuple-element.18.refs_1_.own_in, ...), custom_call_target="tpu_custom_call" | custom-call | flops 2000000 | bytes 2000000 | tf_op jit(solution)/shard_map/weigh/pallas_call | solution.py:341
  65.5 5.4 %collective-permute-start.5 = (f32[16,10,8,128]{3,2,1,0:T(8,128)S(1)}, f32[16,10,8,128]{3,2,1,0:T(8,128)S(1)}, u32[]{:S(2)}, u32[]{:S(2)}) collective-permute-start(f32[16,10,8,128]{3,2,1,0:T(8,128)S(1)} %weigh.1), channel_id=1, source_target_pairs={{0,64},{64,128},{128,192},{1,65},{65,129},{129,193},{2,66},{66,130... | collective-permute-start | bytes 1966088 | tf_op jit(solution)/shard_map/ppermute | solution.py:22
  70.9 1.2 %collective-permute-done.1.follow_own = f32[16,10,8,128]{3,2,1,0:T(8,128)S(1)} collective-permute-done((f32[16,10,8,128]{3,2,1,0:T(8,128)S(1)}, f32[16,10,8,128]{3,2,1,0:T(8,128)S(1)}, u32[]{:S(2)}, u32[]{:S(2)}) %collective-permute-start.1) | collective-permute-done | bytes 655392 | tf_op jit(solution)/shard_map/ppermute | solution.py:22
  72.1 4.4 %backward.1 = f32[16,10,8,128]{3,2,1,0:T(8,128)S(1)} custom-call(s32[2]{0:T(128)S(1)} %pad_add_fusion.window, f32[5,5]{1,0:T(8,128)S(1)} %copy-done.1, f32[5,2]{1,0:T(8,128)S(1)} %constant_dynamic-slice_fusion.prec, f32[26,8,128]{2,1,0:T(8,128)S(1)} %collective-permute-done.follow_west.first, f32[16,10,8,128]{3,2,1,0:T(8,128)S(1)} %collective-permute-done.1.follow_own, ...), custom_call_target="tpu_custom_call" | custom-call | flops 12000000 | bytes 14000000 | tf_op jit(solution)/shard_map/backward/pallas_call | solution.py:351
  76.5 1.9 %collective-permute-done.5 = f32[16,10,8,128]{3,2,1,0:T(8,128)S(1)} collective-permute-done((f32[16,10,8,128]{3,2,1,0:T(8,128)S(1)}, f32[16,10,8,128]{3,2,1,0:T(8,128)S(1)}, u32[]{:S(2)}, u32[]{:S(2)}) %collective-permute-start.5) | collective-permute-done | bytes 655392 | tf_op jit(solution)/shard_map/ppermute | solution.py:22
  78.5 0.1 sub.3
  78.5 0.0 copy-start.3
  78.5 0.0 copy-start.4
  78.5 22.2 %all_to_all.11 = f32[16,10,8,128]{3,2,1,0:T(8,128)S(1)} all-to-all(f32[16,10,8,128]{3,2,1,0:T(8,128)S(1)} %sub.3), channel_id=1, replica_groups={{0,1,2,3,4,5,6,7,8,9,10,11,12,13,14,15},{16,17,18,19,20,21,22,23,24,25,..., dimensions={0} | all-to-all | bytes 1310720 | tf_op jit(solution)/shard_map/all_to_all | solution.py:32
  100.8 0.9 multiply_add_fusion
  (13 shorter events, 0.1 us)
Async XLA Ops:
  0.0 50.5 %copy-start = (f32[5,32]{1,0:T(8,128)S(1)}, f32[5,32]{1,0:T(8,128)}, u32[]{:S(2)}) copy-start(f32[5,32]{1,0:T(8,128)} %param.9) | copy-start | bytes 1924
  0.0 1.2 %copy-start.2 = (f32[1,1,5,32,8,128]{5,4,3,2,1,0:T(8,128)S(1)}, f32[1,1,5,32,8,128]{5,4,3,2,1,0:T(8,128)}, u32[]{:S(2)}) copy-start(f32[1,1,5,32,8,128]{5,4,3,2,1,0:T(8,128)} %param.5) | copy-start | bytes 1966084
  47.7 12.8 %copy-start.1 = (f32[5,5]{1,0:T(8,128)S(1)}, f32[5,5]{1,0:T(8,128)}, u32[]{:S(2)}) copy-start(f32[5,5]{1,0:T(8,128)} %coupling.3) | copy-start | bytes 304
  47.8 12.6 %collective-permute-start.3 = (f32[90,8,128]{2,1,0:T(8,128)S(1)}, f32[90,8,128]{2,1,0:T(8,128)S(1)}, u32[]{:S(2)}, u32[]{:S(2)}) collective-permute-start(f32[90,8,128]{2,1,0:T(8,128)S(1)} %get-tuple-element.15), channel_id=1, source_target_pairs={{0,16},{1,17},{2,18},{3,19},{4,20},{5,21},{6,22},{7,23},{8,24},{9,... | collective-permute-start | bytes 1105928 | tf_op jit(solution)/shard_map/ppermute | solution.py:27
  49.1 11.3 %collective-permute-start.4 = (f32[90,8,128]{2,1,0:T(8,128)S(1)}, f32[90,8,128]{2,1,0:T(8,128)S(1)}, u32[]{:S(2)}, u32[]{:S(2)}) collective-permute-start(f32[90,8,128]{2,1,0:T(8,128)S(1)} %get-tuple-element.16), channel_id=1, source_target_pairs={{0,48},{1,49},{2,50},{3,51},{4,52},{5,53},{6,54},{7,55},{8,56},{9,... | collective-permute-start | bytes 1105928 | tf_op jit(solution)/shard_map/ppermute | solution.py:27
  50.6 13.8 %collective-permute-start = (f32[26,8,128]{2,1,0:T(8,128)S(1)}, f32[26,8,128]{2,1,0:T(8,128)S(1)}, u32[]{:S(2)}, u32[]{:S(2)}) collective-permute-start(f32[26,8,128]{2,1,0:T(8,128)S(1)} %get-tuple-element.13), channel_id=1, source_target_pairs={{64,16},{65,17},{66,18},{67,19},{68,20},{69,21},{70,22},{71,23},{7... | collective-permute-start | bytes 319496 | tf_op jit(solution)/shard_map/ppermute | solution.py:279
  55.8 8.7 %collective-permute-start.2 = (f32[26,8,128]{2,1,0:T(8,128)S(1)}, f32[26,8,128]{2,1,0:T(8,128)S(1)}, u32[]{:S(2)}, u32[]{:S(2)}) collective-permute-start(f32[26,8,128]{2,1,0:T(8,128)S(1)} %get-tuple-element.14), channel_id=1, source_target_pairs={{64,48},{65,49},{66,50},{67,51},{68,52},{69,53},{70,54},{71,55},{7... | collective-permute-start | bytes 319496 | tf_op jit(solution)/shard_map/ppermute | solution.py:279
  58.5 13.7 %collective-permute-start.1 = (f32[16,10,8,128]{3,2,1,0:T(8,128)S(1)}, f32[16,10,8,128]{3,2,1,0:T(8,128)S(1)}, u32[]{:S(2)}, u32[]{:S(2)}) collective-permute-start(f32[16,10,8,128]{3,2,1,0:T(8,128)S(1)} %slice.4), channel_id=1, source_target_pairs={{64,0},{128,64},{192,128},{65,1},{129,65},{193,129},{66,2},{130,66... | collective-permute-start | bytes 1966088 | tf_op jit(solution)/shard_map/ppermute | solution.py:22
  65.5 12.9 %collective-permute-start.5 = (f32[16,10,8,128]{3,2,1,0:T(8,128)S(1)}, f32[16,10,8,128]{3,2,1,0:T(8,128)S(1)}, u32[]{:S(2)}, u32[]{:S(2)}) collective-permute-start(f32[16,10,8,128]{3,2,1,0:T(8,128)S(1)} %weigh.1), channel_id=1, source_target_pairs={{0,64},{64,128},{128,192},{1,65},{65,129},{129,193},{2,66},{66,130... | collective-permute-start | bytes 1966088 | tf_op jit(solution)/shard_map/ppermute | solution.py:22
  78.5 22.3 %copy-start.3 = (f32[1,1,5,32,8,128]{5,4,3,2,1,0:T(8,128)S(1)}, f32[1,1,5,32,8,128]{5,4,3,2,1,0:T(8,128)}, u32[]{:S(2)}) copy-start(f32[1,1,5,32,8,128]{5,4,3,2,1,0:T(8,128)} %param.5) | copy-start | bytes 1966084
  78.5 22.3 %copy-start.4 = (f32[1,1,5,32,8,128]{5,4,3,2,1,0:T(8,128)S(1)}, f32[1,1,5,32,8,128]{5,4,3,2,1,0:T(8,128)}, u32[]{:S(2)}) copy-start(f32[1,1,5,32,8,128]{5,4,3,2,1,0:T(8,128)} %param.6) | copy-start | bytes 1966084

commit v3 on v2

--- a/solution.py
+++ b/solution.py
@@ -82,26 +82,30 @@
 
 
 class Received:
-    def __init__(self, west_packed, west_corner, own, east_packed, east_corner, first=0):
-        self.west, self.east = (west_packed, west_corner), (east_packed, east_corner)
-        self.own, self.first, self.planes = own, first, own.shape[1]
+    def __init__(self, west, own, east, first, keep):
+        self.west, self.own, self.east, self.first, self.keep = west, own, east, first, keep
+
+    def halo(self, side, n, whole, k):
+        packed, corner, tail = side
+        if whole:
+            return packed[(TY - 1) * self.keep + k]
+        return packed[n * self.keep + k] if k < self.keep else tail[n, k - self.keep]
 
     def __getitem__(self, at):
         j, k = at[0], self.first + at[1]
         if j < -TY:
             return self.west[1][k]
         if j < 0:
-            return self.west[0][(j + TY) * self.planes + k]
+            return self.halo(self.west, j + TY, j == -1, k)
         if j < GROUP:
             return self.own[j, k]
         if j < GROUP + TY:
-            return self.east[0][(j - GROUP) * self.planes + k]
+            return self.halo(self.east, j - GROUP - 1, j == GROUP, k)
         return self.east[1][k]
 
 
 def tangent_step(levels, sel, coupling, src, winds, step, tiles, emit):
-    @pl.loop(0, levels)
-    def _(lv):
+    for lv in range(levels):
         for j in tiles:
             u = winds[j, 2 * step * levels + lv]
             v = winds[j, (2 * step + 1) * levels + lv]
@@ -114,8 +118,7 @@
 
 
 def adjoint_step(levels, sel, coupling, src, winds, step, tiles, emit):
-    @pl.loop(0, levels)
-    def _(lv):
+    for lv in range(levels):
         ku = 2 * step * levels + lv
         kv = (2 * step + 1) * levels + lv
         for j in tiles:
@@ -132,8 +135,7 @@
 
 
 def precision_step(levels, sel, prec, src, tiles, emit):
-    @pl.loop(0, levels)
-    def _(lv):
+    for lv in range(levels):
         for j in tiles:
             for a in range(VARS):
                 k = a * levels + lv
@@ -172,16 +174,30 @@
         out[k] = pltpu.roll(packed[at + k // SLOTS], (-CORNER * (k % SLOTS) - shift) % 128, 1)
 
 
+def kept(fields):
+    tail = 2 * fields // VARS
+    return fields + (STEPS - 1) * tail, tail
+
+
 def pack_kernel(fields, own, east_going, west_going, follow_east_going, follow_west_going):
-    top = lax.broadcasted_iota(jnp.int32, (8, 128), 0) < 4
+    row = lax.broadcasted_iota(jnp.int32, (8, 128), 0)
+    top = row < 4
     count = own.shape[1]
+    keep, tail = kept(fields)
     half = fields // 2
-    for out, follow_out, first, paired, whole, corner, shift in (
-        (east_going, follow_east_going, GROUP - TY, GROUP - TY, GROUP - 1, GROUP - HALO, CORNER),
-        (west_going, follow_west_going, 0, 1, 0, TY, 0),
+    for out, follow_out, paired, whole, corner, shift in (
+        (east_going, follow_east_going, GROUP - TY, GROUP - 1, GROUP - HALO, CORNER),
+        (west_going, follow_west_going, 1, 0, TY, 0),
     ):
-        for n in range(TY):
-            out[pl.ds(n * count, count)] = own[first + n]
+        for n in range(TY - 1):
+            out[pl.ds(n * keep, keep)] = own[paired + n, pl.ds(0, keep)]
+            for k in range(tail):
+                last = own[paired + n, keep + k]
+                for step, turn in enumerate((2, 4) if shift else (6, 4)):
+                    at = fields + step * tail + k
+                    free = row < 2 if shift else row >= 6
+                    out[n * keep + at] = jnp.where(free, pltpu.roll(last, turn, 0), own[paired + n, at])
+        out[pl.ds((TY - 1) * keep, count)] = own[whole]
         follow_out[pl.ds((TY - 1) * half, fields)] = own[whole, pl.ds(0, fields)]
         for n in range(TY - 1):
             for k in range(0, fields, 2):
@@ -192,7 +208,7 @@
                     pair = jnp.where(top, one, pltpu.roll(two, 4, 0))
                 follow_out[n * half + k // 2] = pair
         tile = [own[corner, k] for k in range(count)]
-        pack_corner(tile, out, TY * count, shift)
+        pack_corner(tile, out, (TY - 1) * keep + count, shift)
         pack_corner(tile[:fields], follow_out, (TY + 1) * half, shift)
 
 
@@ -203,17 +219,26 @@
     return emit
 
 
-def received(west_in, own_in, east_in, west_corner, east_corner, first):
-    at = TY * own_in.shape[1]
+def received(west_in, own_in, east_in, scratch, fields):
+    row = lax.broadcasted_iota(jnp.int32, (8, 128), 0)
+    keep, tail = kept(fields)
+    west_corner, east_corner, west_tail, east_tail = scratch
+    at = (TY - 1) * keep + own_in.shape[1]
     unpack_corner(west_in, at, west_corner, CORNER)
     unpack_corner(east_in, at, east_corner, 0)
-    return [Received(west_in, west_corner, own_in, east_in, east_corner, f) for f in (0, first)]
+    for n in range(TY - 1):
+        for k in range(tail):
+            one, two = n * keep + fields + k, n * keep + fields + tail + k
+            west_tail[n, k] = jnp.where(row >= 6, pltpu.roll(west_in[one], 6, 0), pltpu.roll(west_in[two], 4, 0))
+            east_tail[n, k] = jnp.where(row < 2, pltpu.roll(east_in[one], 2, 0), pltpu.roll(east_in[two], 4, 0))
+    west, east = (west_in, west_corner, west_tail), (east_in, east_corner, east_tail)
+    return [Received(west, own_in, east, first, keep) for first in (0, fields)]
 
 
 def forward_kernel(levels, window, coupling, prec, west_in, own_in, east_in, *refs):
     sel = masks()
     moved, own_weighted, f0, f1 = Slab(refs[:3]), refs[3], Slab(refs[4:7]), Slab(refs[7:10])
-    state, winds = received(west_in, own_in, east_in, *refs[10:12], VARS * levels)
+    state, winds = received(west_in, own_in, east_in, refs[10:14], VARS * levels)
 
     @pl.when(window[0] != window[1])
     def _():
@@ -234,7 +259,7 @@
     sel = masks()
     moved, own_weighted, out = Slab(refs[:3]), refs[3], refs[7]
     f0, f1 = Slab(refs[8:11]), Slab(refs[11:14])
-    _, winds = received(*refs[4:7], *refs[14:16], VARS * levels)
+    _, winds = received(*refs[4:7], refs[14:18], VARS * levels)
     fields = VARS * levels
 
     @pl.when(window[0] == window[1])
@@ -311,7 +336,8 @@
         return jax.ShapeDtypeStruct((n,) + cell, jnp.float32)
 
     count = slab.shape[1]
-    packed = flat(TY * count + pl.cdiv(count, SLOTS))
+    keep, tail = kept(fields)
+    packed = flat((TY - 1) * keep + count + pl.cdiv(count, SLOTS))
     follow_packed = flat((TY + 1) * (fields // 2) + pl.cdiv(fields, SLOTS))
     east_going, west_going, follow_east_going, follow_west_going = pl.pallas_call(
         functools.partial(pack_kernel, fields),
@@ -327,13 +353,13 @@
         passed_along(slab[:, :fields], "win", -1),
         from_following(follow_west_going, -GROUP),
     )
-    corner = pltpu.VMEM((count,) + cell, jnp.float32)
+    unpacked = [pltpu.VMEM((count,) + cell, jnp.float32)] * 2 + [pltpu.VMEM((TY - 1, tail) + cell, jnp.float32)] * 2
     *moved, own_weighted = pl.pallas_call(
         functools.partial(forward_kernel, levels),
         out_shape=slab_shapes + (core_shape,),
         in_specs=[smem] * 3 + [vmem] * 3,
         out_specs=(vmem,) * 4,
-        scratch_shapes=slab_scratch * 2 + [corner] * 2,
+        scratch_shapes=slab_scratch * 2 + unpacked,
         compiler_params=params,
         cost_estimate=cost(10_000_000, 12_000_000),
         name="forward",
@@ -353,7 +379,7 @@
         out_shape=core_shape,
         in_specs=[smem] * 3 + [vmem] * 10,
         out_specs=vmem,
-        scratch_shapes=slab_scratch * 2 + [corner] * 2,
+        scratch_shapes=slab_scratch * 2 + unpacked,
         compiler_params=params,
         cost_estimate=cost(12_000_000, 14_000_000),
         name="backward",

time: 102 us -> 100 us (0.980)
  blocking collectives: 68.4 us -> 66.1 us
    all_to_all x2, blocking collectives: 68.4 us -> 66.1 us  [exchange(): return lax.all_to_all(x, 'tile', 0, 0, axis_index_groups=groups, tiled=True)]
where the time goes in v3:
time: 100 us; the launch traced here: 99.7 us
  blocking collectives  66.1 us (66%)
  starting transfers between devices  17.8 us (18%)
  Pallas kernels  9.07 us (9%)
  waiting for transfers between devices  3.82 us (4%)
  other arithmetic  2.33 us (2%)
    all_to_all x2, blocking collectives, exchange(): return lax.all_to_all(x, 'tile', 0, 0, axis_index_groups=groups, tiled=True)  66.1 us
    ppermute x2, starting transfers between devices, from_following(): return lax.ppermute(x, ('win', 'tile'), pairs)  7.72 us
    ppermute x2, starting transfers between devices, passed_along(): return lax.ppermute(x, axis, pairs)  7.32 us
    pallas_call x1, Pallas kernels, body(): pl.pallas_call(functools.partial(backward_kernel, levels), out_shape=core...  4.15 us
    ppermute x2, waiting for transfers between devices, passed_along(): return lax.ppermute(x, axis, pairs)  3.81 us
    pallas_call x1, Pallas kernels, body(): pl.pallas_call(functools.partial(forward_kernel, levels), out_shape=slab_...  3.78 us
    ppermute x2, starting transfers between devices, shifted(): lax.ppermute(x, axis, [(i, (i + by) % devices) for i in range(devices)])  2.75 us
  transfers between devices with their start and end apart: 6, of which 2 were waited for; matrix products, arithmetic and copies ran while one was open for 0% of the time, Pallas kernels for 9%

profile of v3, /device:TPU:1, one launch (start us, length us, event | category | flops | bytes accessed | tf_op | source)
XLA Modules:
  0.0 99.7 jit_solution(1599656708392312921)
XLA Ops:
  0.0 1.1 %convert.1 = f32[6,16,2,8,128]{4,3,2,1,0:T(8,128)S(1)} convert(bf16[6,16,2,8,128]{4,3,2,1,0:T(8,128)(2,1)} %bitcast.15) | non-fusion elementwise | flops 196608 | bytes 1179648 | tf_op jit(solution)/shard_map/convert_element_type | solution.py:311
  1.1 0.1 copy-done.2
  1.2 0.1 pad_maximum_fusion
  1.3 0.1 copy.9
  1.4 46.2 %all_to_all.10.own.own_in.refs_5_ = f32[16,22,8,128]{3,2,1,0:T(8,128)S(1)} all-to-all(f32[16,22,8,128]{3,2,1,0:T(8,128)S(1)} %bitcast.11), channel_id=1, replica_groups={{0,1,2,3,4,5,6,7,8,9,10,11,12,13,14,15},{16,17,18,19,20,21,22,23,24,25,..., dimensions={0} | all-to-all | bytes 2883584 | tf_op jit(solution)/shard_map/all_to_all | solution.py:32
  47.7 0.1 pack.1
  47.8 1.3 %collective-permute-start.3 = (f32[78,8,128]{2,1,0:T(8,128)S(1)}, f32[78,8,128]{2,1,0:T(8,128)S(1)}, u32[]{:S(2)}, u32[]{:S(2)}) collective-permute-start(f32[78,8,128]{2,1,0:T(8,128)S(1)} %get-tuple-element.15), channel_id=1, source_target_pairs={{0,16},{1,17},{2,18},{3,19},{4,20},{5,21},{6,22},{7,23},{8,24},{9,... | collective-permute-start | bytes 958472 | tf_op jit(solution)/shard_map/ppermute | solution.py:27
  49.1 1.5 %collective-permute-start.4 = (f32[78,8,128]{2,1,0:T(8,128)S(1)}, f32[78,8,128]{2,1,0:T(8,128)S(1)}, u32[]{:S(2)}, u32[]{:S(2)}) collective-permute-start(f32[78,8,128]{2,1,0:T(8,128)S(1)} %get-tuple-element.16), channel_id=1, source_target_pairs={{0,48},{1,49},{2,50},{3,51},{4,52},{5,53},{6,54},{7,55},{8,56},{9,... | collective-permute-start | bytes 958472 | tf_op jit(solution)/shard_map/ppermute | solution.py:27
  50.5 0.1 constant_dynamic-slice_fusion.prec
  50.6 5.2 %collective-permute-start = (f32[26,8,128]{2,1,0:T(8,128)S(1)}, f32[26,8,128]{2,1,0:T(8,128)S(1)}, u32[]{:S(2)}, u32[]{:S(2)}) collective-permute-start(f32[26,8,128]{2,1,0:T(8,128)S(1)} %get-tuple-element.13), channel_id=1, source_target_pairs={{64,16},{65,17},{66,18},{67,19},{68,20},{69,21},{70,22},{71,23},{7... | collective-permute-start | bytes 319496 | tf_op jit(solution)/shard_map/ppermute | solution.py:304
  55.8 2.6 %collective-permute-start.2 = (f32[26,8,128]{2,1,0:T(8,128)S(1)}, f32[26,8,128]{2,1,0:T(8,128)S(1)}, u32[]{:S(2)}, u32[]{:S(2)}) collective-permute-start(f32[26,8,128]{2,1,0:T(8,128)S(1)} %get-tuple-element.14), channel_id=1, source_target_pairs={{64,48},{65,49},{66,50},{67,51},{68,52},{69,53},{70,54},{71,55},{7... | collective-permute-start | bytes 319496 | tf_op jit(solution)/shard_map/ppermute | solution.py:304
  58.3 0.1 pad_add_fusion.window
  58.5 1.9 %collective-permute-start.1 = (f32[16,10,8,128]{3,2,1,0:T(8,128)S(1)}, f32[16,10,8,128]{3,2,1,0:T(8,128)S(1)}, u32[]{:S(2)}, u32[]{:S(2)}) collective-permute-start(f32[16,10,8,128]{3,2,1,0:T(8,128)S(1)} %slice.4), channel_id=1, source_target_pairs={{64,0},{128,64},{192,128},{65,1},{129,65},{193,129},{66,2},{130,66... | collective-permute-start | bytes 1966088 | tf_op jit(solution)/shard_map/ppermute | solution.py:22
  60.4 0.0 collective-permute-done.3.west_in.refs_4_
  60.4 3.8 %forward.1 = (f32[5,10,8,128]{3,2,1,0:T(8,128)S(1)}, f32[16,10,8,128]{3,2,1,0:T(8,128)S(1)}, f32[5,10,8,128]{3,2,1,0:T(8,128)S(1)}, f32[16,10,8,128]{3,2,1,0:T(8,128)S(1)}) custom-call(s32[2]{0:T(128)S(1)} %pad_add_fusion.window, f32[5,5]{1,0:T(8,128)S(1)} %copy-done.1, f32[5,2]{1,0:T(8,128)S(1)} %constant_dynamic-slice_fusion.prec, ...), custom_call_target="tpu_custom_call" | custom-call | flops 10000000 | bytes 12000000 | tf_op jit(solution)/shard_map/forward/pallas_call | solution.py:357
  64.2 1.0 %weigh.1 = f32[16,10,8,128]{3,2,1,0:T(8,128)S(1)} custom-call(s32[2]{0:T(128)S(1)} %pad_add_fusion.window, f32[5,2]{1,0:T(8,128)S(1)} %constant_dynamic-slice_fusion.prec, f32[5,10,8,128]{3,2,1,0:T(8,128)S(1)} %get-tuple-element.17.refs_0_.west_in, f32[16,10,8,128]{3,2,1,0:T(8,128)S(1)} %get-tuple-element.18.refs_1_.own_in, ...), custom_call_target="tpu_custom_call" | custom-call | flops 2000000 | bytes 2000000 | tf_op jit(solution)/shard_map/weigh/pallas_call | solution.py:367
  65.2 5.4 %collective-permute-start.5 = (f32[16,10,8,128]{3,2,1,0:T(8,128)S(1)}, f32[16,10,8,128]{3,2,1,0:T(8,128)S(1)}, u32[]{:S(2)}, u32[]{:S(2)}) collective-permute-start(f32[16,10,8,128]{3,2,1,0:T(8,128)S(1)} %weigh.1), channel_id=1, source_target_pairs={{0,64},{64,128},{128,192},{1,65},{65,129},{129,193},{2,66},{66,130... | collective-permute-start | bytes 1966088 | tf_op jit(solution)/shard_map/ppermute | solution.py:22
  70.7 1.5 %collective-permute-done.1.follow_own = f32[16,10,8,128]{3,2,1,0:T(8,128)S(1)} collective-permute-done((f32[16,10,8,128]{3,2,1,0:T(8,128)S(1)}, f32[16,10,8,128]{3,2,1,0:T(8,128)S(1)}, u32[]{:S(2)}, u32[]{:S(2)}) %collective-permute-start.1) | collective-permute-done | bytes 655392 | tf_op jit(solution)/shard_map/ppermute | solution.py:22
  72.1 4.1 %backward.1 = f32[16,10,8,128]{3,2,1,0:T(8,128)S(1)} custom-call(s32[2]{0:T(128)S(1)} %pad_add_fusion.window, f32[5,5]{1,0:T(8,128)S(1)} %copy-done.1, f32[5,2]{1,0:T(8,128)S(1)} %constant_dynamic-slice_fusion.prec, f32[26,8,128]{2,1,0:T(8,128)S(1)} %collective-permute-done.follow_west.first, f32[16,10,8,128]{3,2,1,0:T(8,128)S(1)} %collective-permute-done.1.follow_own, ...), custom_call_target="tpu_custom_call" | custom-call | flops 12000000 | bytes 14000000 | tf_op jit(solution)/shard_map/backward/pallas_call | solution.py:377
  76.3 2.3 %collective-permute-done.5 = f32[16,10,8,128]{3,2,1,0:T(8,128)S(1)} collective-permute-done((f32[16,10,8,128]{3,2,1,0:T(8,128)S(1)}, f32[16,10,8,128]{3,2,1,0:T(8,128)S(1)}, u32[]{:S(2)}, u32[]{:S(2)}) %collective-permute-start.5) | collective-permute-done | bytes 655392 | tf_op jit(solution)/shard_map/ppermute | solution.py:22
  78.6 0.1 sub.3
  78.7 0.0 copy-start.4
  78.7 19.9 %all_to_all.11 = f32[16,10,8,128]{3,2,1,0:T(8,128)S(1)} all-to-all(f32[16,10,8,128]{3,2,1,0:T(8,128)S(1)} %sub.3), channel_id=1, replica_groups={{0,1,2,3,4,5,6,7,8,9,10,11,12,13,14,15},{16,17,18,19,20,21,22,23,24,25,..., dimensions={0} | all-to-all | bytes 1310720 | tf_op jit(solution)/shard_map/all_to_all | solution.py:32
  98.7 0.9 multiply_add_fusion
  (13 shorter events, 0.1 us)
Async XLA Ops:
  0.0 50.5 %copy-start = (f32[5,32]{1,0:T(8,128)S(1)}, f32[5,32]{1,0:T(8,128)}, u32[]{:S(2)}) copy-start(f32[5,32]{1,0:T(8,128)} %param.9) | copy-start | bytes 1924
  0.0 1.2 %copy-start.2 = (f32[1,1,5,32,8,128]{5,4,3,2,1,0:T(8,128)S(1)}, f32[1,1,5,32,8,128]{5,4,3,2,1,0:T(8,128)}, u32[]{:S(2)}) copy-start(f32[1,1,5,32,8,128]{5,4,3,2,1,0:T(8,128)} %param.5) | copy-start | bytes 1966084
  47.7 12.8 %copy-start.1 = (f32[5,5]{1,0:T(8,128)S(1)}, f32[5,5]{1,0:T(8,128)}, u32[]{:S(2)}) copy-start(f32[5,5]{1,0:T(8,128)} %coupling.3) | copy-start | bytes 304
  47.8 12.6 %collective-permute-start.3 = (f32[78,8,128]{2,1,0:T(8,128)S(1)}, f32[78,8,128]{2,1,0:T(8,128)S(1)}, u32[]{:S(2)}, u32[]{:S(2)}) collective-permute-start(f32[78,8,128]{2,1,0:T(8,128)S(1)} %get-tuple-element.15), channel_id=1, source_target_pairs={{0,16},{1,17},{2,18},{3,19},{4,20},{5,21},{6,22},{7,23},{8,24},{9,... | collective-permute-start | bytes 958472 | tf_op jit(solution)/shard_map/ppermute | solution.py:27
  49.1 11.3 %collective-permute-start.4 = (f32[78,8,128]{2,1,0:T(8,128)S(1)}, f32[78,8,128]{2,1,0:T(8,128)S(1)}, u32[]{:S(2)}, u32[]{:S(2)}) collective-permute-start(f32[78,8,128]{2,1,0:T(8,128)S(1)} %get-tuple-element.16), channel_id=1, source_target_pairs={{0,48},{1,49},{2,50},{3,51},{4,52},{5,53},{6,54},{7,55},{8,56},{9,... | collective-permute-start | bytes 958472 | tf_op jit(solution)/shard_map/ppermute | solution.py:27
  50.6 13.6 %collective-permute-start = (f32[26,8,128]{2,1,0:T(8,128)S(1)}, f32[26,8,128]{2,1,0:T(8,128)S(1)}, u32[]{:S(2)}, u32[]{:S(2)}) collective-permute-start(f32[26,8,128]{2,1,0:T(8,128)S(1)} %get-tuple-element.13), channel_id=1, source_target_pairs={{64,16},{65,17},{66,18},{67,19},{68,20},{69,21},{70,22},{71,23},{7... | collective-permute-start | bytes 319496 | tf_op jit(solution)/shard_map/ppermute | solution.py:304
  55.8 8.4 %collective-permute-start.2 = (f32[26,8,128]{2,1,0:T(8,128)S(1)}, f32[26,8,128]{2,1,0:T(8,128)S(1)}, u32[]{:S(2)}, u32[]{:S(2)}) collective-permute-start(f32[26,8,128]{2,1,0:T(8,128)S(1)} %get-tuple-element.14), channel_id=1, source_target_pairs={{64,48},{65,49},{66,50},{67,51},{68,52},{69,53},{70,54},{71,55},{7... | collective-permute-start | bytes 319496 | tf_op jit(solution)/shard_map/ppermute | solution.py:304
  58.5 13.7 %collective-permute-start.1 = (f32[16,10,8,128]{3,2,1,0:T(8,128)S(1)}, f32[16,10,8,128]{3,2,1,0:T(8,128)S(1)}, u32[]{:S(2)}, u32[]{:S(2)}) collective-permute-start(f32[16,10,8,128]{3,2,1,0:T(8,128)S(1)} %slice.4), channel_id=1, source_target_pairs={{64,0},{128,64},{192,128},{65,1},{129,65},{193,129},{66,2},{130,66... | collective-permute-start | bytes 1966088 | tf_op jit(solution)/shard_map/ppermute | solution.py:22
  65.2 13.4 %collective-permute-start.5 = (f32[16,10,8,128]{3,2,1,0:T(8,128)S(1)}, f32[16,10,8,128]{3,2,1,0:T(8,128)S(1)}, u32[]{:S(2)}, u32[]{:S(2)}) collective-permute-start(f32[16,10,8,128]{3,2,1,0:T(8,128)S(1)} %weigh.1), channel_id=1, source_target_pairs={{0,64},{64,128},{128,192},{1,65},{65,129},{129,193},{2,66},{66,130... | collective-permute-start | bytes 1966088 | tf_op jit(solution)/shard_map/ppermute | solution.py:22
  78.7 20.0 %copy-start.3 = (f32[1,1,5,32,8,128]{5,4,3,2,1,0:T(8,128)S(1)}, f32[1,1,5,32,8,128]{5,4,3,2,1,0:T(8,128)}, u32[]{:S(2)}) copy-start(f32[1,1,5,32,8,128]{5,4,3,2,1,0:T(8,128)} %param.5) | copy-start | bytes 1966084
  78.7 20.0 %copy-start.4 = (f32[1,1,5,32,8,128]{5,4,3,2,1,0:T(8,128)S(1)}, f32[1,1,5,32,8,128]{5,4,3,2,1,0:T(8,128)}, u32[]{:S(2)}) copy-start(f32[1,1,5,32,8,128]{5,4,3,2,1,0:T(8,128)} %param.6) | copy-start | bytes 1966084
